TPU v7x, 256 devices: a whole 4x4x8 slice. The times are simulated.
256 devices in a mesh: dp: 8 (over z), seq: 2 (over core), hid: 16 (over y, x).
Axes of the slice: x: 4, y: 4, z: 8, core: 2. Of those that a mesh axis runs over, the one named last changes fastest.
Arguments:
- tokens: bfloat16 [2, 4096, 4096], P(None, 'hid', ('dp', 'seq')), may hold values from -6 to 6
- cotangent: bfloat16 [2, 4096, 4096], P(None, 'hid', ('dp', 'seq')), may hold values from -6 to 6
- first_factors: bfloat16 [3, 3, 64, 64, 64], P(None, None, 'hid'), may hold values from -0.75 to 0.75
- second_factors: bfloat16 [3, 3, 64, 64, 64], P(None, None, 'hid'), may hold values from -0.75 to 0.75
- conv_taps: bfloat16 [3, 4, 4096], P(None, None, 'hid'), may hold values from -3 to 3
Outputs:
- input_grad: bfloat16 [2, 4096, 4096], P(None, 'hid', ('dp', 'seq'))
- first_grads: bfloat16 [3, 3, 64, 64, 64], P(None, None, 'hid')
- second_grads: bfloat16 [3, 3, 64, 64, 64], P(None, None, 'hid')
- tap_grads: bfloat16 [3, 4, 4096], P(None, None, 'hid')
All inputs are finite; a program needn't handle non-finite values.
Results may differ from a plain program's by a relative error of at most 0.023.
Values may be sent and summed in bfloat16 or wider, within the bound.
A program may use at most 128 MiB of HBM per device.

v0:
```python
import functools
import math

import jax
import jax.numpy as jnp
from jax import lax
from jax.experimental import pallas as pl
from jax.experimental.pallas import tpu as pltpu
from jax.sharding import PartitionSpec as P

MESH = pl.DeviceIdType.MESH
BF = jnp.bfloat16
F32 = jnp.float32
LANES = 128
ROWS = 32


def iota(shape, dim):
    return lax.broadcasted_iota(jnp.int32, shape, dim)


def nn(a, b):
    return lax.dot_general(a, b, (((1,), (0,)), ((), ())), preferred_element_type=F32)


def nt(a, b):
    return lax.dot_general(a, b, (((1,), (1,)), ((), ())), preferred_element_type=F32)


def ones_where(condition):
    return jnp.where(condition, 1.0, 0.0).astype(BF)


def kernel(
    dims,
    tok,
    cot,
    first,
    second,
    taps,
    out_x,
    out_first,
    out_second,
    out_taps,
    c_exp1,
    c_exp2,
    c_mask1,
    c_mask1t,
    c_mask2,
    c_mask2t,
    c_perm,
    c_permt,
    c_pack1,
    c_pack2,
    w_p,
    w_pt,
    w_qf,
    w_qb,
    w_taps,
    xs,
    us,
    gs,
    opened,
    convolved,
    upo,
    upq,
    flow,
    cb,
    s_q,
    r_q,
    s_o,
    r_o,
    z_o,
    t_o,
    z_q,
    t_q,
    h_fs,
    h_fr,
    h_bs,
    h_br,
    tap_acc,
    g_out,
    g_in,
    g_sum,
    tp_out,
    tp_in,
    tap_total,
    reg_send,
    reg_recv,
    edge_send,
    edge_recv,
    sum_send,
    sum_recv,
):
    layers, ntaps, batch, chan, width, nb, nh, nz, ns = dims
    nx = int(math.isqrt(nh))
    ny = nh // nx
    parts = nz * ns
    block = chan // nh
    share = chan // parts
    pair = 2 * nb
    scale = 1.0 / math.sqrt(batch * parts * width)

    me_h = lax.axis_index("hid")
    me_y, me_x = me_h // nx, me_h % nx
    me_p = lax.axis_index("dp") * ns + lax.axis_index("seq")

    def hid_peer(k):
        return ((me_y + k // nx) % ny) * nx + (me_x + k % nx) % nx

    def part_at(p):
        return {"dp": p // ns, "seq": p % ns}

    def part_peer(k):
        return (me_p + k) % parts

    barrier = pltpu.get_barrier_semaphore()

    def greet_hid(k, _):
        pl.semaphore_signal(barrier, inc=1, device_id={"hid": hid_peer(k)}, device_id_type=MESH)
        return 0

    def greet_part(k, _):
        pl.semaphore_signal(
            barrier, inc=1, device_id=part_at(part_peer(k)), device_id_type=MESH
        )
        return 0

    lax.fori_loop(1, nh, greet_hid, 0)
    lax.fori_loop(1, parts, greet_part, 0)

    lb_shift = 2
    nb_shift = nb.bit_length() - 1
    r_c = iota((chan, nb), 0)
    k_c = iota((chan, nb), 1)
    c_exp1[...] = ones_where(k_c == ((r_c >> 4) << lb_shift) + (r_c & 3))
    c_exp2[...] = ones_where(k_c == (r_c & (nb - 1)))
    r_s = iota((chan, chan), 0)
    c_s = iota((chan, chan), 1)
    c_mask1[...] = ones_where(((c_s >> 2) & 3) == (r_s >> nb_shift))
    c_mask1t[...] = ones_where(((r_s >> 2) & 3) == (c_s >> nb_shift))
    c_mask2[...] = ones_where((r_s & 3) == (c_s >> nb_shift))
    c_mask2t[...] = ones_where((c_s & 3) == (r_s >> nb_shift))
    c_perm[...] = ones_where(c_s == ((r_s & 3) << nb_shift) + (r_s >> 2))
    c_permt[...] = ones_where(r_s == ((c_s & 3) << nb_shift) + (c_s >> 2))
    r_p = iota((chan, pair), 0)
    k_p = iota((chan, pair), 1)
    c_pack1[...] = ones_where(k_p == ((r_p >> 4) << lb_shift) + (r_p & 3))
    c_pack2[...] = ones_where(k_p == nb + (r_p & (nb - 1)))

    def make_pt(i):
        w_pt[i] = nt(c_exp1[...], first[i]).astype(BF) * c_mask1t[...]

    def make_p(i):
        w_p[i] = nt(first[i], c_exp1[...]).astype(BF) * c_mask1[...]

    def make_q(i):
        rows = nn(c_perm[...], second[i]).astype(BF)
        w_qb[i] = nt(rows, c_exp2[...]).astype(BF) * c_mask2[...]
        w_qf[i] = nt(c_exp2[...], rows).astype(BF) * c_mask2t[...]

    def make_taps(layer):
        same = ones_where(iota((chan, chan), 0) == iota((chan, chan), 1))
        columns = nt(same, taps[layer]).astype(BF)
        lane = iota((ntaps, ntaps * LANES), 1) >> 7
        spread = ones_where(lane == iota((ntaps, ntaps * LANES), 0))
        w_taps[layer] = nn(columns, spread)

    def regroup_sem(kind, layer, b):
        return (kind * layers + layer) * batch + b

    def regroup_start(source, target, kind, layer, b):
        sem = regroup_sem(kind, layer, b)
        own = pl.ds(pl.multiple_of(me_h * block, block), block)
        target[layer, b, own, :] = source[layer, b, own, :]

        def send(k, _):
            peer = hid_peer(k)
            pltpu.make_async_remote_copy(
                src_ref=source.at[layer, b, pl.ds(pl.multiple_of(peer * block, block), block)],
                dst_ref=target.at[layer, b, own],
                send_sem=reg_send.at[sem],
                recv_sem=reg_recv.at[sem],
                device_id={"hid": peer},
                device_id_type=MESH,
            ).start()
            return 0

        lax.fori_loop(1, nh, send, 0)

    def regroup_copy(source, target, kind, layer, b):
        sem = regroup_sem(kind, layer, b)
        rest = pl.ds(0, (nh - 1) * block)
        return pltpu.make_async_remote_copy(
            src_ref=source.at[layer, b, rest],
            dst_ref=target.at[layer, b, rest],
            send_sem=reg_send.at[sem],
            recv_sem=reg_recv.at[sem],
            device_id={"hid": hid_peer(1)},
            device_id_type=MESH,
        )

    def edge_copy(source, target, kind, layer, b, step):
        sem = (kind * layers + layer) * batch + b
        return pltpu.make_async_remote_copy(
            src_ref=source.at[layer, b],
            dst_ref=target.at[layer, b],
            send_sem=edge_send.at[sem],
            recv_sem=edge_recv.at[sem],
            device_id=part_at((me_p + step + parts) % parts),
            device_id_type=MESH,
        )

    def scatter_start(source, target, sem, layer):
        own = pl.ds(pl.multiple_of(me_p * share, share), share)
        target[layer, own, :] = source[layer, own, :]

        def send(k, _):
            peer = part_peer(k)
            pltpu.make_async_remote_copy(
                src_ref=source.at[layer, pl.ds(pl.multiple_of(peer * share, share), share)],
                dst_ref=target.at[layer, own],
                send_sem=sum_send.at[sem],
                recv_sem=sum_recv.at[sem],
                device_id=part_at(peer),
                device_id_type=MESH,
            ).start()
            return 0

        lax.fori_loop(1, parts, send, 0)

    def gather_start(target, sem, layer):
        own = pl.ds(pl.multiple_of(me_p * share, share), share)

        def send(k, _):
            pltpu.make_async_remote_copy(
                src_ref=target.at[layer, own],
                dst_ref=target.at[layer, own],
                send_sem=sum_send.at[sem],
                recv_sem=sum_recv.at[sem],
                device_id=part_at(part_peer(k)),
                device_id_type=MESH,
            ).start()
            return 0

        lax.fori_loop(1, parts, send, 0)

    def sum_copy(source, target, sem, layer):
        rest = pl.ds(0, (parts - 1) * share)
        return pltpu.make_async_remote_copy(
            src_ref=source.at[layer, rest],
            dst_ref=target.at[layer, rest],
            send_sem=sum_send.at[sem],
            recv_sem=sum_recv.at[sem],
            device_id=part_at(part_peer(1)),
            device_id_type=MESH,
        )

    def taps_start():
        own = pl.ds(pl.multiple_of(me_p * 16, 16), 16)

        def send(k, _):
            pltpu.make_async_remote_copy(
                src_ref=tp_out,
                dst_ref=tp_in.at[own],
                send_sem=sum_send.at[2 * layers],
                recv_sem=sum_recv.at[2 * layers],
                device_id=part_at(part_peer(k)),
                device_id_type=MESH,
            ).start()
            return 0

        tp_in[own, :] = tp_out[...]
        lax.fori_loop(1, parts, send, 0)

    def taps_copy():
        rest = pl.ds(0, (parts - 1) * 16)
        return pltpu.make_async_remote_copy(
            src_ref=tp_in.at[rest],
            dst_ref=tp_in.at[rest],
            send_sem=sum_send.at[2 * layers],
            recv_sem=sum_recv.at[2 * layers],
            device_id=part_at(part_peer(1)),
            device_id_type=MESH,
        )

    def in_rows(step):
        def one(r, _):
            step(pl.ds(pl.multiple_of(r * ROWS, ROWS), ROWS))
            return 0

        lax.fori_loop(0, chan // ROWS, one, 0)

    has_before = jnp.where(me_p > 0, 1.0, 0.0).astype(F32)
    has_after = jnp.where(me_p < parts - 1, 1.0, 0.0).astype(F32)

    def f1(b, layer):
        x = xs[layer, b]
        s_q[layer, b, :, :width] = nn(w_pt[3 * layer], x).astype(BF)
        s_q[layer, b, :, width:] = nn(w_pt[3 * layer + 1], x).astype(BF)
        regroup_start(s_q, r_q, 0, layer, b)

    def f2(b, layer):
        regroup_copy(s_q, r_q, 0, layer, b).wait_recv()
        signal = nn(w_qf[3 * layer + 1], r_q[layer, b, :, width:]).astype(BF)
        us[layer, b] = signal
        h_fs[layer, b] = signal[:, width - LANES :]
        edge_copy(h_fs, h_fr, 0, layer, b, 1).start()
        query = nn(w_qf[3 * layer], r_q[layer, b, :, :width]).astype(BF).astype(F32)
        opened[layer, b] = jax.nn.sigmoid(query)

    def f3(b, layer):
        edge_copy(h_fs, h_fr, 0, layer, b, 1).wait_recv()

        def step(rows):
            before = h_fr[layer, b, rows, :].astype(F32) * has_before
            signal = us[layer, b, rows, :].astype(F32)
            extended = jnp.concatenate((before, signal), axis=1)
            total = jnp.zeros((ROWS, width), F32)
            for i in range(ntaps):
                tap = w_taps[layer, rows, i * LANES : (i + 1) * LANES]
                tap = jnp.concatenate([tap] * (width // LANES), axis=1)
                moved = signal if i == 0 else pltpu.roll(extended, i, 1)[:, LANES:]
                total = total + tap * moved
            convolved[layer, b, rows, :] = total
            gs[layer, b, rows, :] = (opened[layer, b, rows, :] * total).astype(BF)

        in_rows(step)
        s_o[layer, b] = nn(w_pt[3 * layer + 2], gs[layer, b]).astype(BF)
        regroup_start(s_o, r_o, 1, layer, b)

    def f4(b, layer):
        regroup_copy(s_o, r_o, 1, layer, b).wait_recv()
        if layer + 1 < layers:
            branch = nn(w_qf[3 * layer + 2], r_o[layer, b])
            xs[layer + 1, b] = (xs[layer, b].astype(F32) + branch).astype(BF)

    def b1(b, layer):
        if layer == layers - 1:
            upstream = cot[b]
        else:
            upstream = flow[b].astype(BF)
        upo[layer, b] = upstream
        z_o[layer, b] = nn(w_qb[3 * layer + 2], upstream).astype(BF)
        regroup_start(z_o, t_o, 2, layer, b)

    def b2(b, layer):
        regroup_copy(z_o, t_o, 2, layer, b).wait_recv()
        cb[b] = nn(w_p[3 * layer + 2], t_o[layer, b])

        def step(rows):
            back = cb[b, rows, :]
            gate = opened[layer, b, rows, :]
            conv_back = back * gate
            cb[b, rows, :] = conv_back
            h_bs[layer, b, rows, :] = conv_back[:, :LANES].astype(BF)
            upq[layer, b, rows, :width] = (
                conv_back * convolved[layer, b, rows, :] * (1.0 - gate)
            ).astype(BF)

        in_rows(step)
        edge_copy(h_bs, h_br, 1, layer, b, -1).start()

    def b3(b, layer):
        edge_copy(h_bs, h_br, 1, layer, b, -1).wait_recv()

        def step(rows):
            after = h_br[layer, b, rows, :].astype(F32) * has_after
            conv_back = cb[b, rows, :]
            extended = jnp.concatenate((conv_back, after), axis=1)
            signal = us[layer, b, rows, :].astype(F32)
            total = jnp.zeros((ROWS, width), F32)
            for i in range(ntaps):
                tap = w_taps[layer, rows, i * LANES : (i + 1) * LANES]
                tap = jnp.concatenate([tap] * (width // LANES), axis=1)
                if i == 0:
                    moved = conv_back
                else:
                    moved = pltpu.roll(extended, width + LANES - i, 1)[:, :width]
                total = total + tap * moved
                term = moved * signal
                narrow = term[:, :LANES]
                for q in range(1, width // LANES):
                    narrow = narrow + term[:, q * LANES : (q + 1) * LANES]
                lanes = slice(i * LANES, (i + 1) * LANES)
                if b > 0:
                    narrow = narrow + tap_acc[rows, lanes]
                tap_acc[rows, lanes] = narrow
            upq[layer, b, rows, width:] = total.astype(BF)

        in_rows(step)
        z_q[layer, b, :, :width] = nn(w_qb[3 * layer], upq[layer, b, :, :width]).astype(BF)
        z_q[layer, b, :, width:] = nn(w_qb[3 * layer + 1], upq[layer, b, :, width:]).astype(BF)
        regroup_start(z_q, t_q, 3, layer, b)

    def b4(b, layer):
        regroup_copy(z_q, t_q, 3, layer, b).wait_recv()
        back = nn(w_p[3 * layer], t_q[layer, b, :, :width]) + nn(
            w_p[3 * layer + 1], t_q[layer, b, :, width:]
        )
        before = cot[b].astype(F32) if layer == layers - 1 else flow[b]
        if layer > 0:
            flow[b] = before + back
        else:
            out_x[b] = (before + back).astype(BF)

    def tap_rows(layer):
        total = jnp.zeros((16, chan), F32)
        for i in range(ntaps):
            part = tap_acc[:, i * LANES : (i + 1) * LANES]
            high = part.astype(BF)
            low = (part - high.astype(F32)).astype(BF)
            row = ones_where(iota((16, LANES), 0) == layer * ntaps + i)
            total = total + nt(row, high) + nt(row, low)
        if layer == layers - 1:
            tap_total[...] = total
        else:
            tap_total[...] += total

    def grads(layer, m, inputs, spread, sections, upstream):
        one = nt(inputs[0], spread[0])
        two = nt(sections[0], upstream[0])
        for b in range(1, batch):
            one = one + nt(inputs[b], spread[b])
            two = two + nt(sections[b], upstream[b])
        packed = nn(one.astype(BF) * c_mask1[...], c_pack1[...])
        other = nn(two.astype(BF) * c_mask2[...], c_pack2[...]).astype(BF)
        packed = packed + nn(c_permt[...], other)
        g_out[layer, :, m * pair : (m + 1) * pair] = packed.astype(BF)

    both = range(batch)

    def grads_o(layer):
        grads(
            layer,
            2,
            [gs[layer, b] for b in both],
            [t_o[layer, b] for b in both],
            [r_o[layer, b] for b in both],
            [upo[layer, b] for b in both],
        )

    def grads_in(layer):
        for m in range(2):
            lanes = slice(m * width, (m + 1) * width)
            grads(
                layer,
                m,
                [xs[layer, b] for b in both],
                [t_q[layer, b, :, lanes] for b in both],
                [r_q[layer, b, :, lanes] for b in both],
                [upq[layer, b, :, lanes] for b in both],
            )
        scatter_start(g_out, g_in, layer, layer)

    def total_up(layer):
        sum_copy(g_out, g_in, layer, layer).wait_recv()
        total = g_in[layer, :share, :].astype(F32)
        for p in range(1, parts):
            total = total + g_in[layer, p * share : (p + 1) * share, :].astype(F32)
        own = pl.ds(pl.multiple_of(me_p * share, share), share)
        g_sum[layer, own, :] = (total * scale).astype(BF)
        gather_start(g_sum, layers + layer, layer)

    def finish(layer):
        sum_copy(g_sum, g_sum, layers + layer, layer).wait_recv()
        for m in range(3):
            out_first[3 * layer + m] = g_sum[layer, :, m * pair : m * pair + nb]
            out_second[3 * layer + m] = g_sum[layer, :, m * pair + nb : (m + 1) * pair]

    for b in both:
        xs[0, b] = tok[b]
    make_pt(0)
    make_pt(1)
    pl.semaphore_wait(barrier, nh - 1 + parts - 1)
    for b in both:
        f1(b, 0)
    for i in range(3):
        make_q(i)
    make_pt(2)
    make_taps(0)
    for layer in range(layers):
        for b in both:
            f2(b, layer)
        if layer + 1 < layers:
            for m in range(3):
                make_q(3 * layer + 3 + m)
                make_pt(3 * layer + 3 + m)
            make_taps(layer + 1)
        for b in both:
            f3(b, layer)
        for m in range(3):
            make_p(3 * layer + m)
        if layer == layers - 1:
            for b in both:
                b1(b, layer)
        for b in both:
            f4(b, layer)
            if layer + 1 < layers:
                f1(b, layer + 1)
    for layer in reversed(range(layers)):
        for b in both:
            b2(b, layer)
        for b in both:
            b3(b, layer)
        tap_rows(layer)
        grads_o(layer)
        if layer == 0:
            tp_out[...] = tap_total[...].astype(BF)
            taps_start()
        if layer + 1 < layers:
            total_up(layer + 1)
        for b in both:
            b4(b, layer)
            if layer > 0:
                b1(b, layer - 1)
        grads_in(layer)
        if layer + 1 < layers:
            finish(layer + 1)
    taps_copy().wait_recv()
    total = tp_in[:16, :].astype(F32)
    for p in range(1, parts):
        total = total + tp_in[p * 16 : (p + 1) * 16, :].astype(F32)
    total = (total * scale).astype(BF)
    for layer in range(layers):
        out_taps[layer] = total[layer * ntaps : (layer + 1) * ntaps, :]
    total_up(0)
    finish(0)

    for layer in range(layers):
        for b in both:
            regroup_copy(s_q, r_q, 0, layer, b).wait_send()
            regroup_copy(s_o, r_o, 1, layer, b).wait_send()
            regroup_copy(z_o, t_o, 2, layer, b).wait_send()
            regroup_copy(z_q, t_q, 3, layer, b).wait_send()
            edge_copy(h_fs, h_fr, 0, layer, b, 1).wait_send()
            edge_copy(h_bs, h_br, 1, layer, b, -1).wait_send()
        sum_copy(g_out, g_in, layer, layer).wait_send()
        sum_copy(g_sum, g_sum, layers + layer, layer).wait_send()
    taps_copy().wait_send()


def body(sizes, tokens, cotangent, first_factors, second_factors, conv_taps):
    nh, nz, ns = sizes
    batch, chan, width = tokens.shape
    layers, ntaps, _ = conv_taps.shape
    nb = first_factors.shape[3]
    projections = first_factors.shape[1]
    parts = nz * ns
    share = chan // parts
    pair = 2 * nb
    many = layers * projections
    dims = (layers, ntaps, batch, chan, width, nb, nh, nz, ns)
    V = pltpu.VMEM
    sq = (chan, chan)
    act = (layers, batch, chan, width)
    wide = (layers, batch, chan, 2 * width)
    edge = (layers, batch, chan, LANES)
    grad = (layers, chan, projections * pair)
    scratch = [
        V((chan, nb), BF),
        V((chan, nb), BF),
        V(sq, BF),
        V(sq, BF),
        V(sq, BF),
        V(sq, BF),
        V(sq, BF),
        V(sq, BF),
        V((chan, pair), BF),
        V((chan, pair), BF),
        V((many,) + sq, BF),
        V((many,) + sq, BF),
        V((many,) + sq, BF),
        V((many,) + sq, BF),
        V((layers, chan, ntaps * LANES), F32),
        V(act, BF),
        V(act, BF),
        V(act, BF),
        V(act, F32),
        V(act, F32),
        V(act, BF),
        V(wide, BF),
        V((batch, chan, width), F32),
        V((batch, chan, width), F32),
        V(wide, BF),
        V(wide, BF),
        V(act, BF),
        V(act, BF),
        V(act, BF),
        V(act, BF),
        V(wide, BF),
        V(wide, BF),
        V(edge, BF),
        V(edge, BF),
        V(edge, BF),
        V(edge, BF),
        V((chan, ntaps * LANES), F32),
        V(grad, BF),
        V((layers, parts * share, projections * pair), BF),
        V(grad, BF),
        V((16, chan), BF),
        V((parts * 16, chan), BF),
        V((16, chan), F32),
        pltpu.SemaphoreType.DMA((4 * layers * batch,)),
        pltpu.SemaphoreType.DMA((4 * layers * batch,)),
        pltpu.SemaphoreType.DMA((2 * layers * batch,)),
        pltpu.SemaphoreType.DMA((2 * layers * batch,)),
        pltpu.SemaphoreType.DMA((2 * layers + 1,)),
        pltpu.SemaphoreType.DMA((2 * layers + 1,)),
    ]
    whole = pl.BlockSpec(memory_space=pltpu.VMEM)
    out_x, out_first, out_second, out_taps = pl.pallas_call(
        functools.partial(kernel, dims),
        out_shape=(
            jax.ShapeDtypeStruct((batch, chan, width), BF),
            jax.ShapeDtypeStruct((many, chan, nb), BF),
            jax.ShapeDtypeStruct((many, chan, nb), BF),
            jax.ShapeDtypeStruct((layers, ntaps, chan), BF),
        ),
        in_specs=[whole] * 5,
        out_specs=[whole] * 4,
        scratch_shapes=scratch,
        compiler_params=pltpu.CompilerParams(
            collective_id=0, has_side_effects=True, vmem_limit_bytes=56 * 1024 * 1024
        ),
    )(
        tokens,
        cotangent,
        first_factors.reshape(many, chan, nb),
        second_factors.reshape(many, chan, nb),
        conv_taps,
    )
    return (
        out_x,
        out_first.reshape(first_factors.shape),
        out_second.reshape(second_factors.shape),
        out_taps,
    )


def solution(mesh):
    sizes = (mesh.shape["hid"], mesh.shape["dp"], mesh.shape["seq"])
    return jax.shard_map(
        functools.partial(body, sizes),
        mesh=mesh,
        in_specs=(
            P(None, "hid", ("dp", "seq")),
            P(None, "hid", ("dp", "seq")),
            P(None, None, "hid", None, None),
            P(None, None, "hid", None, None),
            P(None, None, "hid"),
        ),
        out_specs=(
            P(None, "hid", ("dp", "seq")),
            P(None, None, "hid", None, None),
            P(None, None, "hid", None, None),
            P(None, None, "hid"),
        ),
        check_vma=False,
    )
```

profile of v0, /device:TPU:1, one launch (start us, length us, event | category | flops | bytes accessed | tf_op | source)
XLA Modules:
  0.0 132.5 jit_solution(913350220807013543)
XLA Ops:
  0.6 126.8 %shard_map.84 = (bf16[2,256,256]{2,1,0:T(8,128)(2,1)}, bf16[9,256,64]{2,1,0:T(8,128)(2,1)}, bf16[9,256,64]{2,1,0:T(8,128)(2,1)}, bf16[3,4,256]{2,1,0:T(4,128)(2,1)}) custom-call(bf16[2,256,256]{2,1,0:T(8,128)(2,1)} %tok.1, bf16[2,256,256]{2,1,0:T(8,128)(2,1)} %cot.1, bf16[9,256,64]{2,1,0:T(8,128)(2,1)} %bitcast.6, bf16[9,256,64]{2,1,0:T(8,128)(2,1)} %bitcast.7, ...), custom_call_target="tpu_custom_call" | custom-call | tf_op jit(solution)/shard_map/pallas_call | solution.py:612
  127.4 1.7 %copy.13 = bf16[2,256,256]{2,1,0:T(8,128)(2,1)} copy(bf16[2,256,256]{2,1,0:T(8,128)(2,1)} %get-tuple-element.16) | data formatting | bytes 524288
  129.1 0.0 copy-start
  129.1 2.0 %copy.14 = bf16[3,3,4,64,64]{4,3,2,1,0:T(8,128)(2,1)} copy(bf16[3,3,4,64,64]{4,3,2,1,0:T(8,128)(2,1)} %bitcast.5) | data formatting | bytes 589824
  131.0 0.0 copy-done
  131.1 0.0 copy-start.1
  131.1 0.8 copy.15
  131.9 0.0 copy-done.1
  131.9 0.6 copy.16
Async XLA Ops:
  129.1 2.0 %copy-start = (bf16[9,256,64]{2,1,0:T(8,128)(2,1)S(1)}, bf16[9,256,64]{2,1,0:T(8,128)(2,1)}, u32[]{:S(2)}) copy-start(bf16[9,256,64]{2,1,0:T(8,128)(2,1)} %get-tuple-element.10) | copy-start | bytes 884740
  131.1 0.8 copy-start.1
where the time goes:
time: 133 us; the launch traced here: 132 us
  Pallas kernels  127 us (95%)
  local copies, waits for them, and re-layouts  5.06 us (4%)
    pallas_call x1, Pallas kernels, body(): pl.pallas_call(functools.partial(kernel, dims), out_shape=(jax.ShapeDtype...  127 us
    unnamed x8, local copies, waits for them, and re-layouts  5.06 us

commit v1 on v0

v1 whole, which is shorter than its diff:
```python
import functools
import math

import jax
import jax.numpy as jnp
from jax import lax
from jax.experimental import pallas as pl
from jax.experimental.pallas import tpu as pltpu
from jax.sharding import PartitionSpec as P

MESH = pl.DeviceIdType.MESH
BF = jnp.bfloat16
F32 = jnp.float32
LANES = 128
ROWS = 32


def iota(shape, dim):
    return lax.broadcasted_iota(jnp.int32, shape, dim)


def nn(a, b):
    return lax.dot_general(a, b, (((1,), (0,)), ((), ())), preferred_element_type=F32)


def nt(a, b):
    return lax.dot_general(a, b, (((1,), (1,)), ((), ())), preferred_element_type=F32)


def ones_where(condition):
    return jnp.where(condition, 1.0, 0.0).astype(BF)


def kernel(
    dims,
    tok,
    cot,
    first,
    second,
    taps,
    out_x,
    g_sum,
    out_taps,
    c_exp1,
    c_exp2,
    c_mask1,
    c_mask1t,
    c_mask2,
    c_mask2t,
    c_perm,
    c_permt,
    c_pack1,
    c_pack2,
    c_same,
    w_p,
    w_pt,
    w_qf,
    w_qb,
    w_taps,
    xs,
    us,
    gs,
    opened,
    convolved,
    ups,
    flow,
    cb,
    sent,
    got,
    edge_out,
    edge_in,
    edge_wide,
    tap_acc,
    g_out,
    g_in,
    tp_out,
    tp_in,
    tap_total,
    reg_send,
    reg_recv,
    edge_send,
    edge_recv,
    sum_send,
    sum_recv,
):
    layers, ntaps, batch, chan, width, nb, nh, nz, ns = dims
    nx = int(math.isqrt(nh))
    ny = nh // nx
    parts = nz * ns
    block = chan // nh
    share = chan // parts
    pair = 2 * nb
    scale = 1.0 / math.sqrt(batch * parts * width)

    me_h = lax.axis_index("hid")
    me_y, me_x = me_h // nx, me_h % nx
    me_z, me_c = lax.axis_index("dp"), lax.axis_index("seq")
    me_p = me_z * ns + me_c

    def far(k, n):
        return min(k, n - k)

    def hid_at(h):
        return (me_z, me_c, h)

    def part_at(p):
        return (p // ns, p % ns, me_h)

    turns = [(dy, dx) for dy in range(ny) for dx in range(nx) if dy + dx > 0]
    turns.sort(key=lambda t: -far(t[0], ny) - far(t[1], nx))
    peers_y = [(me_y + dy) % ny * nx for dy in range(ny)]
    peers_x = [(me_x + dx) % nx for dx in range(nx)]
    hid_peers = [peers_y[dy] + peers_x[dx] for dy, dx in turns]
    steps = sorted(range(1, parts), key=lambda k: -far(k, parts))
    part_peers = [(me_p + k) % parts for k in steps]
    part_ids = [part_at(p) for p in part_peers]

    barrier = pltpu.get_barrier_semaphore()

    for h in hid_peers:
        pl.semaphore_signal(barrier, inc=1, device_id=hid_at(h), device_id_type=MESH)
    for where in part_ids:
        pl.semaphore_signal(barrier, inc=1, device_id=where, device_id_type=MESH)

    nb_shift = nb.bit_length() - 1
    r_c, k_c = iota((chan, nb), 0), iota((chan, nb), 1)
    r_s, c_s = iota((chan, chan), 0), iota((chan, chan), 1)
    r_p, k_p = iota((chan, pair), 0), iota((chan, pair), 1)

    def constants_first():
        c_exp1[...] = ones_where(k_c == ((r_c >> 4) << 2) + (r_c & 3))
        c_mask1t[...] = ones_where(((r_s >> 2) & 3) == (c_s >> nb_shift))

    def constants_second():
        c_exp2[...] = ones_where(k_c == (r_c & (nb - 1)))
        c_perm[...] = ones_where(c_s == ((r_s & 3) << nb_shift) + (r_s >> 2))
        c_mask2[...] = ones_where((r_s & 3) == (c_s >> nb_shift))
        c_mask2t[...] = ones_where((c_s & 3) == (r_s >> nb_shift))
        c_same[...] = ones_where(r_s == c_s)

    def constants_last():
        c_mask1[...] = ones_where(((c_s >> 2) & 3) == (r_s >> nb_shift))
        c_permt[...] = ones_where(r_s == ((c_s & 3) << nb_shift) + (c_s >> 2))
        for half in range(2):
            to1 = half * nb + ((r_p >> 4) << 2) + (r_p & 3)
            c_pack1[half] = ones_where(k_p == to1)
            c_pack2[half] = ones_where(k_p == half * nb + (r_p & (nb - 1)))

    def make_pt(i):
        w_pt[i] = nt(c_exp1[...], first[i]).astype(BF) * c_mask1t[...]

    def make_p(i):
        w_p[i] = nt(first[i], c_exp1[...]).astype(BF) * c_mask1[...]

    def make_q(i):
        rows = nn(c_perm[...], second[i]).astype(BF)
        w_qb[i] = nt(rows, c_exp2[...]).astype(BF) * c_mask2[...]
        w_qf[i] = nt(c_exp2[...], rows).astype(BF) * c_mask2t[...]

    def make_taps(layer):
        columns = nt(c_same[...], taps[layer]).astype(BF)
        lane = iota((ntaps, ntaps * LANES), 1) >> 7
        spread = ones_where(lane == iota((ntaps, ntaps * LANES), 0))
        w_taps[layer] = nn(columns, spread)

    own_rows = pl.ds(pl.multiple_of(me_h * block, block), block)

    def at(kind, layer, b):
        return (kind * layers + layer) * batch + b

    def regroup_start(i):
        got[i, own_rows, :] = sent[i, own_rows, :]

        for peer in hid_peers:
            pltpu.make_async_remote_copy(
                src_ref=sent.at[i, pl.ds(pl.multiple_of(peer * block, block), block)],
                dst_ref=got.at[i, own_rows],
                send_sem=reg_send.at[i],
                recv_sem=reg_recv.at[i],
                device_id=hid_at(peer),
                device_id_type=MESH,
            ).start()

    def regroup_copy(i):
        rest = pl.ds(0, (nh - 1) * block)
        return pltpu.make_async_remote_copy(
            src_ref=sent.at[i, rest],
            dst_ref=got.at[i, rest],
            send_sem=reg_send.at[i],
            recv_sem=reg_recv.at[i],
            device_id=hid_at(hid_peers[0]),
            device_id_type=MESH,
        )

    edge = ntaps - 1

    def edge_copy(kind, layer, b):
        i = at(kind, layer, b)
        step = steps.index(1 if kind == 0 else parts - 1)
        return pltpu.make_async_remote_copy(
            src_ref=edge_out.at[i],
            dst_ref=edge_in.at[i],
            send_sem=edge_send.at[i],
            recv_sem=edge_recv.at[i],
            device_id=part_ids[step],
            device_id_type=MESH,
        )

    e_r, e_l = iota((16, LANES), 0), iota((16, LANES), 1)

    def edge_start(kind, layer, b, columns):
        lane = e_r + (LANES - edge) if kind == 0 else e_r
        pick = ones_where((e_r < edge) & (e_l == lane))
        edge_out[at(kind, layer, b)] = nt(pick, columns).astype(BF)
        edge_copy(kind, layer, b).start()

    def edge_finish(kind, layer, b):
        edge_copy(kind, layer, b).wait_recv()
        lane = e_r + (LANES - edge) if kind == 0 else e_r
        there = (me_p > 0) if kind == 0 else (me_p < parts - 1)
        keep = jnp.where(there, 1.0, 0.0).astype(F32)
        pick = ones_where((e_r < edge) & (e_l == lane))
        columns = nt(c_same[...], edge_in[at(kind, layer, b)]).astype(BF)
        edge_wide[kind] = nn(columns, pick) * keep

    own_share = pl.ds(pl.multiple_of(me_p * share, share), share)
    late = layers

    def lanes_of(i):
        if i == late:
            return 0, pl.ds(2 * pair, pair)
        if i == 0:
            return 0, pl.ds(0, 2 * pair)
        return i, pl.ds(0, 3 * pair)

    def share_start(i, source, target, mine):
        layer, lanes = lanes_of(i)

        for peer, where in zip(part_peers, part_ids):
            away = pl.ds(pl.multiple_of(peer * share, share), share)
            pltpu.make_async_remote_copy(
                src_ref=source.at[layer, own_share if mine else away, lanes],
                dst_ref=target.at[layer, own_share, lanes],
                send_sem=sum_send.at[2 * i + mine],
                recv_sem=sum_recv.at[2 * i + mine],
                device_id=where,
                device_id_type=MESH,
            ).start()

    def share_copy(i, source, target, mine):
        layer, lanes = lanes_of(i)
        rest = pl.ds(0, (parts - 1) * share)
        return pltpu.make_async_remote_copy(
            src_ref=source.at[layer, rest, lanes],
            dst_ref=target.at[layer, rest, lanes],
            send_sem=sum_send.at[2 * i + mine],
            recv_sem=sum_recv.at[2 * i + mine],
            device_id=part_ids[0],
            device_id_type=MESH,
        )

    def scatter_start(i):
        layer, lanes = lanes_of(i)
        g_in[layer, own_share, lanes] = g_out[layer, own_share, lanes]
        share_start(i, g_out, g_in, 0)

    def total_up(i):
        share_copy(i, g_out, g_in, 0).wait_recv()
        layer, lanes = lanes_of(i)
        total = g_in[layer, pl.ds(0, share), lanes].astype(F32)
        for p in range(1, parts):
            total = total + g_in[layer, pl.ds(p * share, share), lanes].astype(F32)
        g_sum[layer, own_share, lanes] = (total * scale).astype(BF)
        share_start(i, g_sum, g_sum, 1)

    def taps_start():
        own = pl.ds(pl.multiple_of(me_p * 16, 16), 16)

        tp_in[own, :] = tp_out[...]
        for where in part_ids:
            pltpu.make_async_remote_copy(
                src_ref=tp_out,
                dst_ref=tp_in.at[own],
                send_sem=sum_send.at[2 * layers + 2],
                recv_sem=sum_recv.at[2 * layers + 2],
                device_id=where,
                device_id_type=MESH,
            ).start()

    def taps_copy():
        rest = pl.ds(0, (parts - 1) * 16)
        return pltpu.make_async_remote_copy(
            src_ref=tp_in.at[rest],
            dst_ref=tp_in.at[rest],
            send_sem=sum_send.at[2 * layers + 2],
            recv_sem=sum_recv.at[2 * layers + 2],
            device_id=part_ids[0],
            device_id_type=MESH,
        )

    def in_rows(step):
        def one(r, _):
            step(pl.ds(pl.multiple_of(r * ROWS, ROWS), ROWS))
            return 0

        lax.fori_loop(0, chan // ROWS, one, 0, unroll=True)

    u_f, q_f, o_f, o_b, q_b, u_b = range(6)
    last = layers - 1
    cut = width - LANES

    def stream(b, layer):
        return tok[b] if layer == 0 else xs[layer, b]

    def f1_one(b, layer, m, kind):
        sent[at(kind, layer, b)] = nn(w_pt[3 * layer + m], stream(b, layer)).astype(BF)

    def f1(b, layer):
        for m, kind in ((1, u_f), (0, q_f)):
            f1_one(b, layer, m, kind)
            regroup_start(at(kind, layer, b))

    def f2_signal(b, layer):
        i = at(u_f, layer, b)
        regroup_copy(i).wait_recv()
        tail = nn(w_qf[3 * layer + 1], got[i, :, cut:]).astype(BF)
        edge_start(0, layer, b, tail)
        us[layer, b, :, cut:] = tail
        us[layer, b, :, :cut] = nn(w_qf[3 * layer + 1], got[i, :, :cut]).astype(BF)

    def f2_query(b, layer):
        i = at(q_f, layer, b)
        regroup_copy(i).wait_recv()
        query = nn(w_qf[3 * layer], got[i]).astype(BF).astype(F32)
        opened[layer, b] = jax.nn.sigmoid(query)

    def f3(b, layer):
        edge_finish(0, layer, b)

        def step(rows):
            signal = us[layer, b, rows, :].astype(F32)
            extended = jnp.concatenate((edge_wide[0, rows, :], signal), axis=1)
            total = jnp.zeros((ROWS, width), F32)
            for i in range(ntaps):
                tap = w_taps[layer, rows, i * LANES : (i + 1) * LANES]
                tap = jnp.concatenate([tap] * (width // LANES), axis=1)
                moved = signal if i == 0 else pltpu.roll(extended, i, 1)[:, LANES:]
                total = total + tap * moved
            convolved[layer, b, rows, :] = total
            gs[layer, b, rows, :] = (opened[layer, b, rows, :] * total).astype(BF)

        in_rows(step)

    def f3_send(b, layer):
        i = at(o_f, layer, b)
        sent[i] = nn(w_pt[3 * layer + 2], gs[layer, b]).astype(BF)
        regroup_start(i)

    def f4(b, layer):
        i = at(o_f, layer, b)
        regroup_copy(i).wait_recv()
        if layer < last:
            branch = nn(w_qf[3 * layer + 2], got[i])
            xs[layer + 1, b] = (stream(b, layer).astype(F32) + branch).astype(BF)

    def b1_spread(b, layer):
        upstream = cot[b] if layer == last else flow[b].astype(BF)
        ups[at(0, layer, b)] = upstream
        sent[at(o_b, layer, b)] = nn(w_qb[3 * layer + 2], upstream).astype(BF)

    def b1(b, layer):
        b1_spread(b, layer)
        regroup_start(at(o_b, layer, b))

    def gated_back(b, layer):
        i = at(o_b, layer, b)
        regroup_copy(i).wait_recv()
        cb[b] = nn(w_p[3 * layer + 2], got[i])

    def b2_edge(b, layer):
        if layer < last:
            i = at(o_b, layer, b)
            regroup_copy(i).wait_recv()
            head = nn(w_p[3 * layer + 2], got[i, :, :LANES])
        else:
            head = cb[b, :, :LANES]
        head = head * opened[layer, b, :, :LANES]
        edge_start(1, layer, b, head.astype(BF))
        cb[b, :, :LANES] = head
        if layer < last:
            rest = nn(w_p[3 * layer + 2], got[i, :, LANES:])
        else:
            rest = cb[b, :, LANES:]
        cb[b, :, LANES:] = rest * opened[layer, b, :, LANES:]

    def b2_query(b, layer):
        def step(rows):
            shut = 1.0 - opened[layer, b, rows, :]
            back = cb[b, rows, :] * convolved[layer, b, rows, :] * shut
            ups[at(1, layer, b), rows, :] = back.astype(BF)

        in_rows(step)
        i = at(q_b, layer, b)
        sent[i] = nn(w_qb[3 * layer], ups[at(1, layer, b)]).astype(BF)
        regroup_start(i)

    def b3(b, layer):
        edge_finish(1, layer, b)

        def step(rows):
            conv_back = cb[b, rows, :]
            extended = jnp.concatenate((conv_back, edge_wide[1, rows, :]), axis=1)
            signal = us[layer, b, rows, :].astype(F32)
            total = jnp.zeros((ROWS, width), F32)
            for i in range(ntaps):
                tap = w_taps[layer, rows, i * LANES : (i + 1) * LANES]
                tap = jnp.concatenate([tap] * (width // LANES), axis=1)
                if i == 0:
                    moved = conv_back
                else:
                    moved = pltpu.roll(extended, width + LANES - i, 1)[:, :width]
                total = total + tap * moved
                term = moved * signal
                narrow = term[:, :LANES]
                for q in range(1, width // LANES):
                    narrow = narrow + term[:, q * LANES : (q + 1) * LANES]
                lanes = slice(i * LANES, (i + 1) * LANES)
                if b > 0:
                    narrow = narrow + tap_acc[rows, lanes]
                tap_acc[rows, lanes] = narrow
            ups[at(2, layer, b), rows, :] = total.astype(BF)

        in_rows(step)
        i = at(u_b, layer, b)
        sent[i] = nn(w_qb[3 * layer + 1], ups[at(2, layer, b)]).astype(BF)
        regroup_start(i)

    def b4(b, layer):
        regroup_copy(at(q_b, layer, b)).wait_recv()
        regroup_copy(at(u_b, layer, b)).wait_recv()
        back = nn(w_p[3 * layer], got[at(q_b, layer, b)])
        back = back + nn(w_p[3 * layer + 1], got[at(u_b, layer, b)])
        before = cot[b].astype(F32) if layer == last else flow[b]
        if layer > 0:
            flow[b] = before + back
        else:
            out_x[b] = (before + back).astype(BF)

    def tap_rows(layer):
        total = jnp.zeros((16, chan), F32)
        for i in range(ntaps):
            part = tap_acc[:, i * LANES : (i + 1) * LANES]
            high = part.astype(BF)
            low = (part - high.astype(F32)).astype(BF)
            row = ones_where(e_r == layer * ntaps + i)
            total = total + nt(row, high) + nt(row, low)
        if layer == last:
            tap_total[...] = total
        else:
            tap_total[...] += total

    both = range(batch)

    def first_term(half, inputs, spread):
        term = nt(inputs[0], spread[0])
        for b in range(1, batch):
            term = term + nt(inputs[b], spread[b])
        return nn(term.astype(BF) * c_mask1[...], c_pack1[half])

    def second_term(half, sections, upstream):
        term = nt(sections[0], upstream[0])
        for b in range(1, batch):
            term = term + nt(sections[b], upstream[b])
        narrow = nn(term.astype(BF) * c_mask2[...], c_pack2[half]).astype(BF)
        return nn(c_permt[...], narrow)

    def every(ref, kind, layer):
        return [ref[at(kind, layer, b)] for b in both]

    def grads_early(layer):
        second_o = second_term(1, every(got, o_f, layer), every(ups, 0, layer))
        first_o = first_term(0, [gs[layer, b] for b in both], every(got, o_b, layer))
        g_out[layer, :, :pair] = (first_o + second_o).astype(BF)
        second_q = second_term(0, every(got, q_f, layer), every(ups, 1, layer))
        second_u = second_term(1, every(got, u_f, layer), every(ups, 2, layer))
        g_out[layer, :, pair : 2 * pair] = (second_q + second_u).astype(BF)

    def grads_late(layer):
        inputs = [stream(b, layer) for b in both]
        first_q = first_term(0, inputs, every(got, q_b, layer))
        first_u = first_term(1, inputs, every(got, u_b, layer))
        g_out[layer, :, 2 * pair :] = (first_q + first_u).astype(BF)

    constants_first()
    make_pt(1)
    make_pt(0)
    for b in both:
        f1_one(b, 0, 1, u_f)
        f1_one(b, 0, 0, q_f)
    constants_second()
    pl.semaphore_wait(barrier, nh - 1 + parts - 1)
    for b in both:
        regroup_start(at(u_f, 0, b))
        regroup_start(at(q_f, 0, b))
    make_q(3 * last + 2)
    for b in both:
        b1(b, last)
    make_q(1)
    make_q(0)
    make_taps(0)
    make_pt(2)
    make_q(2)
    for layer in range(layers):
        if layer == last:
            for m in range(2):
                make_p(3 * last + m)
        for b in both:
            f2_signal(b, layer)
            if b == 0:
                f2_query(b, layer)
                if layer == last:
                    b2_edge(b, layer)
        for b in both:
            if b > 0:
                f2_query(b, layer)
                if layer == last:
                    b2_edge(b, layer)
            f3(b, layer)
            if layer < last:
                f3_send(b, layer)
            else:
                b2_query(b, layer)
                b3(b, layer)
        if layer < last:
            for m in range(3):
                make_pt(3 * layer + 3 + m)
            for b in both:
                f4(b, layer)
                f1(b, layer + 1)
            for m in range(3):
                if layer + 1 < last or m < 2:
                    make_q(3 * layer + 3 + m)
            make_taps(layer + 1)
            if layer == 0:
                constants_last()
                make_p(3 * last + 2)
                for b in both:
                    gated_back(b, last)
    for b in both:
        f3_send(b, last)
    for layer in reversed(range(layers)):
        if layer < last:
            b2_edge(0, layer)
            b2_query(0, layer)
            for b in range(1, batch):
                b2_edge(b, layer)
            for b in both:
                if b > 0:
                    b2_query(b, layer)
                b3(b, layer)
        tap_rows(layer)
        if layer == 0:
            tp_out[...] = tap_total[...].astype(BF)
            taps_start()
        if layer == last:
            for b in both:
                f4(b, last)
        grads_early(layer)
        if layer == 0:
            scatter_start(0)
        if layer > 0:
            make_p(3 * layer - 1)
            for b in both:
                b4(b, layer)
                b1(b, layer - 1)
            grads_late(layer)
            scatter_start(layer)
            for m in range(2):
                make_p(3 * layer - 3 + m)
        if 0 < layer < last:
            total_up(layer + 1)
    total_up(1)
    for b in both:
        regroup_copy(at(q_b, 0, b)).wait_recv()
        regroup_copy(at(u_b, 0, b)).wait_recv()
    grads_late(0)
    scatter_start(late)
    for b in both:
        back = nn(w_p[0], got[at(q_b, 0, b)]) + nn(w_p[1], got[at(u_b, 0, b)])
        out_x[b] = (flow[b] + back).astype(BF)
    total_up(0)
    taps_copy().wait_recv()
    total = tp_in[:16, :].astype(F32)
    for p in range(1, parts):
        total = total + tp_in[p * 16 : (p + 1) * 16, :].astype(F32)
    total = (total * scale).astype(BF)
    for layer in range(layers):
        out_taps[layer] = total[layer * ntaps : (layer + 1) * ntaps, :]
    total_up(late)

    for i in range(6 * layers * batch):
        regroup_copy(i).wait_send()
    for layer in range(layers):
        for b in both:
            edge_copy(0, layer, b).wait_send()
            edge_copy(1, layer, b).wait_send()
    taps_copy().wait_send()
    for i in range(layers + 1):
        share_copy(i, g_out, g_in, 0).wait_send()
        share_copy(i, g_sum, g_sum, 1).wait()


def unpack(nb, projections, x, sums, tap, out_x, out_first, out_second, out_taps, held, sems):
    load = pltpu.make_async_copy(sums, held, sems.at[0])
    load.start()
    whole_x = pltpu.make_async_copy(x, out_x, sems.at[1])
    whole_x.start()
    out_taps[...] = tap[...]
    load.wait()
    for layer in range(sums.shape[0]):
        for m in range(projections):
            one = (4 + m if m < 2 else 0) * nb
            two = (2 + m if m < 2 else 1) * nb
            out_first[projections * layer + m] = held[layer, :, one : one + nb]
            out_second[projections * layer + m] = held[layer, :, two : two + nb]
    whole_x.wait()


def body(sizes, tokens, cotangent, first_factors, second_factors, conv_taps):
    nh, nz, ns = sizes
    batch, chan, width = tokens.shape
    layers, ntaps, _ = conv_taps.shape
    nb = first_factors.shape[3]
    projections = first_factors.shape[1]
    parts = nz * ns
    share = chan // parts
    pair = 2 * nb
    many = layers * projections
    dims = (layers, ntaps, batch, chan, width, nb, nh, nz, ns)
    V = pltpu.VMEM
    sq = (chan, chan)
    act = (layers, batch, chan, width)
    regroups = 6 * layers * batch
    grad = (layers, chan, projections * pair)
    scratch = [
        V((chan, nb), BF),
        V((chan, nb), BF),
        V(sq, BF),
        V(sq, BF),
        V(sq, BF),
        V(sq, BF),
        V(sq, BF),
        V(sq, BF),
        V((2, chan, pair), BF),
        V((2, chan, pair), BF),
        V(sq, BF),
        V((many,) + sq, BF),
        V((many,) + sq, BF),
        V((many,) + sq, BF),
        V((many,) + sq, BF),
        V((layers, chan, ntaps * LANES), F32),
        V(act, BF),
        V(act, BF),
        V(act, BF),
        V(act, F32),
        V(act, F32),
        V((3 * layers * batch, chan, width), BF),
        V((batch, chan, width), F32),
        V((batch, chan, width), F32),
        V((regroups, chan, width), BF),
        V((regroups, chan, width), BF),
        V((2 * layers * batch, 16, chan), BF),
        V((2 * layers * batch, 16, chan), BF),
        V((2, chan, LANES), F32),
        V((chan, ntaps * LANES), F32),
        V(grad, BF),
        V((layers, parts * share, projections * pair), BF),
        V((16, chan), BF),
        V((parts * 16, chan), BF),
        V((16, chan), F32),
        pltpu.SemaphoreType.DMA((regroups,)),
        pltpu.SemaphoreType.DMA((regroups,)),
        pltpu.SemaphoreType.DMA((2 * layers * batch,)),
        pltpu.SemaphoreType.DMA((2 * layers * batch,)),
        pltpu.SemaphoreType.DMA((2 * layers + 3,)),
        pltpu.SemaphoreType.DMA((2 * layers + 3,)),
    ]
    whole = pl.BlockSpec(memory_space=pltpu.VMEM)
    anywhere = pl.BlockSpec(memory_space=pl.ANY)
    x_shape = jax.ShapeDtypeStruct((batch, chan, width), BF)
    factor_shape = jax.ShapeDtypeStruct((many, chan, nb), BF)
    taps_shape = jax.ShapeDtypeStruct((layers, ntaps, chan), BF)
    moved = pl.pallas_call(
        functools.partial(kernel, dims),
        out_shape=(x_shape, jax.ShapeDtypeStruct(grad, BF), taps_shape),
        in_specs=[whole] * 5,
        out_specs=[whole] * 3,
        scratch_shapes=scratch,
        compiler_params=pltpu.CompilerParams(
            collective_id=0, has_side_effects=True, vmem_limit_bytes=56 * 1024 * 1024
        ),
    )(
        tokens,
        cotangent,
        first_factors.reshape(many, chan, nb),
        second_factors.reshape(many, chan, nb),
        conv_taps,
    )
    out_x, out_first, out_second, out_taps = pl.pallas_call(
        functools.partial(unpack, nb, projections),
        out_shape=(x_shape, factor_shape, factor_shape, taps_shape),
        in_specs=[anywhere, anywhere, whole],
        out_specs=[whole] * 4,
        scratch_shapes=[V(grad, BF), pltpu.SemaphoreType.DMA((2,))],
        compiler_params=pltpu.CompilerParams(vmem_limit_bytes=56 * 1024 * 1024),
    )(*moved)
    return (
        out_x,
        out_first.reshape(first_factors.shape),
        out_second.reshape(second_factors.shape),
        out_taps,
    )


def solution(mesh):
    sizes = (mesh.shape["hid"], mesh.shape["dp"], mesh.shape["seq"])
    return jax.shard_map(
        functools.partial(body, sizes),
        mesh=mesh,
        in_specs=(
            P(None, "hid", ("dp", "seq")),
            P(None, "hid", ("dp", "seq")),
            P(None, None, "hid", None, None),
            P(None, None, "hid", None, None),
            P(None, None, "hid"),
        ),
        out_specs=(
            P(None, "hid", ("dp", "seq")),
            P(None, None, "hid", None, None),
            P(None, None, "hid", None, None),
            P(None, None, "hid"),
        ),
        check_vma=False,
    )
```

time: 133 us -> 113 us (0.85)
  Pallas kernels: 127 us -> 112 us
  local copies, waits for them, and re-layouts: 5.06 us -> 0 us
    pallas_call x1 -> x2, Pallas kernels: 127 us -> 112 us  [the longest x1 109 us: body(): pl.pallas_call(functools.partial(kernel, dims), out_shape=(x_shape, jax.S...]
    unnamed x8 -> x0, local copies, waits for them, and re-layouts: 5.06 us -> none
where the time goes in v1:
time: 113 us
  Pallas kernels  112 us (99%)
    pallas_call x1, Pallas kernels, body(): pl.pallas_call(functools.partial(kernel, dims), out_shape=(x_shape, jax.S...  109 us
    pallas_call x1, Pallas kernels, body(): pl.pallas_call(functools.partial(unpack, nb, projections), out_shape=(x_s...  3.34 us

profile of v1, /device:TPU:1, one launch (start us, length us, event | category | flops | bytes accessed | tf_op | source)
XLA Modules:
  0.0 112.9 jit_solution(11676209241167324919)
XLA Ops:
  0.6 108.8 %shard_map.84 = (bf16[2,256,256]{2,1,0:T(8,128)(2,1)}, bf16[3,256,384]{2,1,0:T(8,128)(2,1)}, bf16[3,4,256]{2,1,0:T(4,128)(2,1)}) custom-call(bf16[2,256,256]{2,1,0:T(8,128)(2,1)} %tok.1, bf16[2,256,256]{2,1,0:T(8,128)(2,1)} %cot.1, bf16[9,256,64]{2,1,0:T(8,128)(2,1)} %bitcast.4, bf16[9,256,64]{2,1,0:T(8,128)(2,1)} %bitcast.5, bf16[3,4,256]{2,1,0:T(4,128)(2,1)} %taps.1), custom_call_target="tpu_custom_call" | custom-call | tf_op jit(solution)/shard_map/pallas_call | solution.py:693
  109.4 3.3 %shard_map.85 = (bf16[2,256,256]{2,1,0:T(8,128)(2,1)}, bf16[9,256,64]{2,1,0:T(8,128)(2,1)}, bf16[9,256,64]{2,1,0:T(8,128)(2,1)}, bf16[3,4,256]{2,1,0:T(4,128)(2,1)}) custom-call(bf16[2,256,256]{2,1,0:T(8,128)(2,1)} %get-tuple-element.11.x, bf16[3,256,384]{2,1,0:T(8,128)(2,1)} %get-tuple-element.12.sums, bf16[3,4,256]{2,1,0:T(4,128)(2,1)} %get-tuple-element.13.tap), custom_call_target="tpu_custom_call" | custom-call | tf_op jit(solution)/shard_map/pallas_call | solution.py:709

commit v2 on v1

--- a/solution.py
+++ b/solution.py
@@ -72,6 +72,8 @@
     edge_wide,
     tap_acc,
     g_out,
+    g_pair,
+    g_half,
     g_in,
     tp_out,
     tp_in,
@@ -224,79 +226,128 @@
         edge_wide[kind] = nn(columns, pick) * keep
 
     own_share = pl.ds(pl.multiple_of(me_p * share, share), share)
-    late = layers
-
-    def lanes_of(i):
-        if i == late:
-            return 0, pl.ds(2 * pair, pair)
-        if i == 0:
-            return 0, pl.ds(0, 2 * pair)
-        return i, pl.ds(0, 3 * pair)
-
-    def share_start(i, source, target, mine):
-        layer, lanes = lanes_of(i)
-
+    half = nz * share
+    own_half = pl.ds(pl.multiple_of(me_c * half, half), half)
+    other_half = pl.ds(pl.multiple_of((ns - 1 - me_c) * half, half), half)
+    own_slot = pl.ds(pl.multiple_of(me_z * share, share), share)
+    own_part = pl.ds(pl.multiple_of(me_c * half + me_z * share, share), share)
+    rest_slots = pl.ds(0, (nz - 1) * share)
+    sibling = (me_z, ns - 1 - me_c, me_h)
+    steps_z = sorted(range(1, nz), key=lambda k: -far(k, nz))
+    peers_z = [(me_z + k) % nz for k in steps_z]
+    late = 4 * layers
+
+    def lanes_of(layer):
+        return pl.ds(0, (2 if layer == 0 else 3) * pair)
+
+    def sum_copy(sem, source, target, where):
+        return pltpu.make_async_remote_copy(
+            src_ref=source,
+            dst_ref=target,
+            send_sem=sum_send.at[sem],
+            recv_sem=sum_recv.at[sem],
+            device_id=where,
+            device_id_type=MESH,
+        )
+
+    def pair_copy(layer):
+        lanes = lanes_of(layer)
+        source = g_out.at[layer, other_half, lanes]
+        return sum_copy(4 * layer, source, g_pair.at[layer, pl.ds(0, half), lanes], sibling)
+
+    def slots_copy(layer):
+        lanes = lanes_of(layer)
+        source = g_half.at[layer, rest_slots, lanes]
+        target = g_in.at[layer, rest_slots, lanes]
+        return sum_copy(4 * layer + 1, source, target, (peers_z[0], me_c, me_h))
+
+    def parts_copy(layer):
+        rows = g_sum.at[layer, rest_slots, lanes_of(layer)]
+        return sum_copy(4 * layer + 2, rows, rows, (peers_z[0], me_c, me_h))
+
+    def back_copy(layer):
+        rows = g_sum.at[layer, own_half, lanes_of(layer)]
+        return sum_copy(4 * layer + 3, rows, rows, sibling)
+
+    def pair_up(layer):
+        pair_copy(layer).wait_recv()
+        lanes = lanes_of(layer)
+        total = g_out[layer, own_half, lanes].astype(F32)
+        total = total + g_pair[layer, pl.ds(0, half), lanes].astype(F32)
+        g_half[layer, pl.ds(0, half), lanes] = total.astype(BF)
+        g_in[layer, own_slot, lanes] = g_half[layer, own_slot, lanes]
+        for z in peers_z:
+            away = pl.ds(pl.multiple_of(z * share, share), share)
+            source = g_half.at[layer, away, lanes]
+            target = g_in.at[layer, own_slot, lanes]
+            sum_copy(4 * layer + 1, source, target, (z, me_c, me_h)).start()
+
+    def total_up(layer):
+        slots_copy(layer).wait_recv()
+        lanes = lanes_of(layer)
+        total = g_in[layer, pl.ds(0, share), lanes].astype(F32)
+        for z in range(1, nz):
+            total = total + g_in[layer, pl.ds(z * share, share), lanes].astype(F32)
+        g_sum[layer, own_part, lanes] = (total * scale).astype(BF)
+        rows = g_sum.at[layer, own_part, lanes]
+        for z in peers_z:
+            sum_copy(4 * layer + 2, rows, rows, (z, me_c, me_h)).start()
+
+    def hand_back(layer):
+        parts_copy(layer).wait_recv()
+        back_copy(layer).start()
+
+    late_lanes = pl.ds(2 * pair, pair)
+
+    def late_copy(source, target, back):
+        rest = pl.ds(0, (parts - 1) * share)
+        one, two = source.at[0, rest, late_lanes], target.at[0, rest, late_lanes]
+        return sum_copy(late + back, one, two, part_ids[0])
+
+    def late_scatter():
+        g_in[0, own_share, late_lanes] = g_out[0, own_share, late_lanes]
+        target = g_in.at[0, own_share, late_lanes]
         for peer, where in zip(part_peers, part_ids):
             away = pl.ds(pl.multiple_of(peer * share, share), share)
-            pltpu.make_async_remote_copy(
-                src_ref=source.at[layer, own_share if mine else away, lanes],
-                dst_ref=target.at[layer, own_share, lanes],
-                send_sem=sum_send.at[2 * i + mine],
-                recv_sem=sum_recv.at[2 * i + mine],
-                device_id=where,
-                device_id_type=MESH,
-            ).start()
-
-    def share_copy(i, source, target, mine):
-        layer, lanes = lanes_of(i)
-        rest = pl.ds(0, (parts - 1) * share)
-        return pltpu.make_async_remote_copy(
-            src_ref=source.at[layer, rest, lanes],
-            dst_ref=target.at[layer, rest, lanes],
-            send_sem=sum_send.at[2 * i + mine],
-            recv_sem=sum_recv.at[2 * i + mine],
-            device_id=part_ids[0],
-            device_id_type=MESH,
-        )
-
-    def scatter_start(i):
-        layer, lanes = lanes_of(i)
-        g_in[layer, own_share, lanes] = g_out[layer, own_share, lanes]
-        share_start(i, g_out, g_in, 0)
-
-    def total_up(i):
-        share_copy(i, g_out, g_in, 0).wait_recv()
-        layer, lanes = lanes_of(i)
-        total = g_in[layer, pl.ds(0, share), lanes].astype(F32)
+            sum_copy(late, g_out.at[0, away, late_lanes], target, where).start()
+
+    def late_total():
+        late_copy(g_out, g_in, 0).wait_recv()
+        total = g_in[0, pl.ds(0, share), late_lanes].astype(F32)
         for p in range(1, parts):
-            total = total + g_in[layer, pl.ds(p * share, share), lanes].astype(F32)
-        g_sum[layer, own_share, lanes] = (total * scale).astype(BF)
-        share_start(i, g_sum, g_sum, 1)
-
-    def taps_start():
+            total = total + g_in[0, pl.ds(p * share, share), late_lanes].astype(F32)
+        g_sum[0, own_share, late_lanes] = (total * scale).astype(BF)
+        rows = g_sum.at[0, own_share, late_lanes]
+        for where in part_ids:
+            sum_copy(late + 1, rows, rows, where).start()
+
+    def taps_start(tile):
         own = pl.ds(pl.multiple_of(me_p * 16, 16), 16)
-
-        tp_in[own, :] = tp_out[...]
+        tp_in[tile, own, :] = tp_out[tile]
         for where in part_ids:
-            pltpu.make_async_remote_copy(
-                src_ref=tp_out,
-                dst_ref=tp_in.at[own],
-                send_sem=sum_send.at[2 * layers + 2],
-                recv_sem=sum_recv.at[2 * layers + 2],
-                device_id=where,
-                device_id_type=MESH,
-            ).start()
-
-    def taps_copy():
-        rest = pl.ds(0, (parts - 1) * 16)
-        return pltpu.make_async_remote_copy(
-            src_ref=tp_in.at[rest],
-            dst_ref=tp_in.at[rest],
-            send_sem=sum_send.at[2 * layers + 2],
-            recv_sem=sum_recv.at[2 * layers + 2],
-            device_id=part_ids[0],
-            device_id_type=MESH,
-        )
+            sum_copy(late + 2 + tile, tp_out.at[tile], tp_in.at[tile, own], where).start()
+
+    def taps_copy(tile):
+        rest = tp_in.at[tile, pl.ds(0, (parts - 1) * 16)]
+        return sum_copy(late + 2 + tile, rest, rest, part_ids[0])
+
+    def taps_total(tile):
+        taps_copy(tile).wait_recv()
+        total = tp_in[tile, pl.ds(0, 16), :].astype(F32)
+        for p in range(1, parts):
+            total = total + tp_in[tile, pl.ds(p * 16, 16), :].astype(F32)
+        total = (total * scale).astype(BF)
+        for layer in range(layers):
+            if (layer == 0) == (tile == 1):
+                for side in range(2):
+                    row = taps_row(layer) + side * ntaps
+                    lanes = slice(side * tap_width, (side + 1) * tap_width)
+                    out_taps[layer, :, lanes] = total[row : row + ntaps, :]
+
+    tap_width = chan // 2
+
+    def taps_row(layer):
+        return 0 if layer == 0 else (layers - 1 - layer) * 2 * ntaps
 
     def in_rows(step):
         def one(r, _):
@@ -447,17 +498,25 @@
             out_x[b] = (before + back).astype(BF)
 
     def tap_rows(layer):
-        total = jnp.zeros((16, chan), F32)
+        total = jnp.zeros((16, tap_width), F32)
         for i in range(ntaps):
-            part = tap_acc[:, i * LANES : (i + 1) * LANES]
-            high = part.astype(BF)
-            low = (part - high.astype(F32)).astype(BF)
-            row = ones_where(e_r == layer * ntaps + i)
-            total = total + nt(row, high) + nt(row, low)
+            for side in range(2):
+                rows = slice(side * tap_width, (side + 1) * tap_width)
+                part = tap_acc[rows, i * LANES : (i + 1) * LANES]
+                high = part.astype(BF)
+                low = (part - high.astype(F32)).astype(BF)
+                row = ones_where(e_r == taps_row(layer) + side * ntaps + i)
+                total = total + nt(row, high) + nt(row, low)
         if layer == last:
             tap_total[...] = total
-        else:
+        elif layer > 0:
             tap_total[...] += total
+        if layer == 1:
+            tp_out[0] = tap_total[...].astype(BF)
+            taps_start(0)
+        if layer == 0:
+            tp_out[1] = total.astype(BF)
+            taps_start(1)
 
     both = range(batch)
 
@@ -477,10 +536,12 @@
     def every(ref, kind, layer):
         return [ref[at(kind, layer, b)] for b in both]
 
-    def grads_early(layer):
+    def grads_o(layer):
         second_o = second_term(1, every(got, o_f, layer), every(ups, 0, layer))
         first_o = first_term(0, [gs[layer, b] for b in both], every(got, o_b, layer))
         g_out[layer, :, :pair] = (first_o + second_o).astype(BF)
+
+    def grads_second(layer):
         second_q = second_term(0, every(got, q_f, layer), every(ups, 1, layer))
         second_u = second_term(1, every(got, u_f, layer), every(ups, 2, layer))
         g_out[layer, :, pair : 2 * pair] = (second_q + second_u).astype(BF)
@@ -559,44 +620,43 @@
                     b2_query(b, layer)
                 b3(b, layer)
         tap_rows(layer)
-        if layer == 0:
-            tp_out[...] = tap_total[...].astype(BF)
-            taps_start()
-        if layer == last:
-            for b in both:
-                f4(b, last)
-        grads_early(layer)
-        if layer == 0:
-            scatter_start(0)
         if layer > 0:
             make_p(3 * layer - 1)
+            grads_second(layer)
+            if layer < last:
+                pair_up(layer + 1)
             for b in both:
                 b4(b, layer)
                 b1(b, layer - 1)
+            if layer == last:
+                for b in both:
+                    f4(b, last)
+            grads_o(layer)
             grads_late(layer)
-            scatter_start(layer)
+            pair_copy(layer).start()
             for m in range(2):
                 make_p(3 * layer - 3 + m)
-        if 0 < layer < last:
-            total_up(layer + 1)
-    total_up(1)
+            if layer < last:
+                total_up(layer + 1)
+        else:
+            grads_o(0)
+            grads_second(0)
+            pair_copy(0).start()
+            pair_up(1)
+            hand_back(2)
+            pair_up(0)
     for b in both:
         regroup_copy(at(q_b, 0, b)).wait_recv()
         regroup_copy(at(u_b, 0, b)).wait_recv()
     grads_late(0)
-    scatter_start(late)
+    late_scatter()
     for b in both:
         back = nn(w_p[0], got[at(q_b, 0, b)]) + nn(w_p[1], got[at(u_b, 0, b)])
         out_x[b] = (flow[b] + back).astype(BF)
+    total_up(1)
     total_up(0)
-    taps_copy().wait_recv()
-    total = tp_in[:16, :].astype(F32)
-    for p in range(1, parts):
-        total = total + tp_in[p * 16 : (p + 1) * 16, :].astype(F32)
-    total = (total * scale).astype(BF)
-    for layer in range(layers):
-        out_taps[layer] = total[layer * ntaps : (layer + 1) * ntaps, :]
-    total_up(late)
+    taps_total(0)
+    taps_total(1)
 
     for i in range(6 * layers * batch):
         regroup_copy(i).wait_send()
@@ -604,10 +664,18 @@
         for b in both:
             edge_copy(0, layer, b).wait_send()
             edge_copy(1, layer, b).wait_send()
-    taps_copy().wait_send()
-    for i in range(layers + 1):
-        share_copy(i, g_out, g_in, 0).wait_send()
-        share_copy(i, g_sum, g_sum, 1).wait()
+        pair_copy(layer).wait_send()
+        slots_copy(layer).wait_send()
+    taps_copy(0).wait_send()
+    taps_copy(1).wait_send()
+    late_total()
+    hand_back(1)
+    hand_back(0)
+    late_copy(g_out, g_in, 0).wait_send()
+    for layer in range(layers):
+        parts_copy(layer).wait_send()
+        back_copy(layer).wait()
+    late_copy(g_sum, g_sum, 1).wait()
 
 
 def unpack(nb, projections, x, sums, tap, out_x, out_first, out_second, out_taps, held, sems):
@@ -674,16 +742,18 @@
         V((2, chan, LANES), F32),
         V((chan, ntaps * LANES), F32),
         V(grad, BF),
+        V((layers, nz * share, projections * pair), BF),
+        V((layers, nz * share, projections * pair), BF),
         V((layers, parts * share, projections * pair), BF),
-        V((16, chan), BF),
-        V((parts * 16, chan), BF),
-        V((16, chan), F32),
+        V((2, 16, chan // 2), BF),
+        V((2, parts * 16, chan // 2), BF),
+        V((16, chan // 2), F32),
         pltpu.SemaphoreType.DMA((regroups,)),
         pltpu.SemaphoreType.DMA((regroups,)),
         pltpu.SemaphoreType.DMA((2 * layers * batch,)),
         pltpu.SemaphoreType.DMA((2 * layers * batch,)),
-        pltpu.SemaphoreType.DMA((2 * layers + 3,)),
-        pltpu.SemaphoreType.DMA((2 * layers + 3,)),
+        pltpu.SemaphoreType.DMA((4 * layers + 4,)),
+        pltpu.SemaphoreType.DMA((4 * layers + 4,)),
     ]
     whole = pl.BlockSpec(memory_space=pltpu.VMEM)
     anywhere = pl.BlockSpec(memory_space=pl.ANY)

time: 113 us -> 104 us (0.920)
  Pallas kernels: 112 us -> 103 us
    pallas_call x1, Pallas kernels: 109 us -> 99.6 us  [body(): pl.pallas_call(functools.partial(kernel, dims), out_shape=(x_shape, jax.S...]
where the time goes in v2:
time: 104 us
  Pallas kernels  103 us (99%)
    pallas_call x1, Pallas kernels, body(): pl.pallas_call(functools.partial(kernel, dims), out_shape=(x_shape, jax.S...  99.6 us
    pallas_call x1, Pallas kernels, body(): pl.pallas_call(functools.partial(unpack, nb, projections), out_shape=(x_s...  3.34 us

profile of v2, /device:TPU:1, one launch (start us, length us, event | category | flops | bytes accessed | tf_op | source)
XLA Modules:
  0.0 103.7 jit_solution(10224996937944144794)
XLA Ops:
  0.6 99.6 %shard_map.84 = (bf16[2,256,256]{2,1,0:T(8,128)(2,1)}, bf16[3,256,384]{2,1,0:T(8,128)(2,1)}, bf16[3,4,256]{2,1,0:T(4,128)(2,1)}) custom-call(bf16[2,256,256]{2,1,0:T(8,128)(2,1)} %tok.1, bf16[2,256,256]{2,1,0:T(8,128)(2,1)} %cot.1, bf16[9,256,64]{2,1,0:T(8,128)(2,1)} %bitcast.4, bf16[9,256,64]{2,1,0:T(8,128)(2,1)} %bitcast.5, bf16[3,4,256]{2,1,0:T(4,128)(2,1)} %taps.1), custom_call_target="tpu_custom_call" | custom-call | tf_op jit(solution)/shard_map/pallas_call | solution.py:763
  100.2 3.3 %shard_map.85 = (bf16[2,256,256]{2,1,0:T(8,128)(2,1)}, bf16[9,256,64]{2,1,0:T(8,128)(2,1)}, bf16[9,256,64]{2,1,0:T(8,128)(2,1)}, bf16[3,4,256]{2,1,0:T(4,128)(2,1)}) custom-call(bf16[2,256,256]{2,1,0:T(8,128)(2,1)} %get-tuple-element.11.x, bf16[3,256,384]{2,1,0:T(8,128)(2,1)} %get-tuple-element.12.sums, bf16[3,4,256]{2,1,0:T(4,128)(2,1)} %get-tuple-element.13.tap), custom_call_target="tpu_custom_call" | custom-call | tf_op jit(solution)/shard_map/pallas_call | solution.py:779

commit v3 on v2

--- a/solution.py
+++ b/solution.py
@@ -33,10 +33,10 @@
 
 def kernel(
     dims,
-    tok,
-    cot,
-    first,
-    second,
+    tok_in,
+    cot_in,
+    first_in,
+    second_in,
     taps,
     out_x,
     g_sum,
@@ -70,6 +70,7 @@
     edge_out,
     edge_in,
     edge_wide,
+    back_tail,
     tap_acc,
     g_out,
     g_pair,
@@ -84,6 +85,11 @@
     edge_recv,
     sum_send,
     sum_recv,
+    tok,
+    cot,
+    first,
+    second,
+    in_sems,
 ):
     layers, ntaps, batch, chan, width, nb, nh, nz, ns = dims
     nx = int(math.isqrt(nh))
@@ -116,6 +122,11 @@
     steps = sorted(range(1, parts), key=lambda k: -far(k, parts))
     part_peers = [(me_p + k) % parts for k in steps]
     part_ids = [part_at(p) for p in part_peers]
+
+    pairs = ((first_in, first), (tok_in, tok), (second_in, second), (cot_in, cot))
+    loads = [pltpu.make_async_copy(a, b, in_sems.at[i]) for i, (a, b) in enumerate(pairs)]
+    for load in loads:
+        load.start()
 
     barrier = pltpu.get_barrier_semaphore()
 
@@ -210,10 +221,13 @@
 
     e_r, e_l = iota((16, LANES), 0), iota((16, LANES), 1)
 
-    def edge_start(kind, layer, b, columns):
+    def edge_start(kind, layer, b, columns, weight=None):
         lane = e_r + (LANES - edge) if kind == 0 else e_r
         pick = ones_where((e_r < edge) & (e_l == lane))
-        edge_out[at(kind, layer, b)] = nt(pick, columns).astype(BF)
+        rows = nt(pick, columns).astype(BF)
+        if weight is not None:
+            rows = nt(rows, weight).astype(BF)
+        edge_out[at(kind, layer, b)] = rows
         edge_copy(kind, layer, b).start()
 
     def edge_finish(kind, layer, b):
@@ -222,8 +236,9 @@
         there = (me_p > 0) if kind == 0 else (me_p < parts - 1)
         keep = jnp.where(there, 1.0, 0.0).astype(F32)
         pick = ones_where((e_r < edge) & (e_l == lane))
-        columns = nt(c_same[...], edge_in[at(kind, layer, b)]).astype(BF)
-        edge_wide[kind] = nn(columns, pick) * keep
+        rows = edge_in[at(kind, layer, b)]
+        wide = lax.dot_general(rows, pick, (((0,), (0,)), ((), ())), preferred_element_type=F32)
+        edge_wide[kind] = wide * keep
 
     own_share = pl.ds(pl.multiple_of(me_p * share, share), share)
     half = nz * share
@@ -374,10 +389,8 @@
     def f2_signal(b, layer):
         i = at(u_f, layer, b)
         regroup_copy(i).wait_recv()
-        tail = nn(w_qf[3 * layer + 1], got[i, :, cut:]).astype(BF)
-        edge_start(0, layer, b, tail)
-        us[layer, b, :, cut:] = tail
-        us[layer, b, :, :cut] = nn(w_qf[3 * layer + 1], got[i, :, :cut]).astype(BF)
+        edge_start(0, layer, b, got[i, :, cut:], w_qf[3 * layer + 1])
+        us[layer, b] = nn(w_qf[3 * layer + 1], got[i]).astype(BF)
 
     def f2_query(b, layer):
         i = at(q_f, layer, b)
@@ -385,26 +398,49 @@
         query = nn(w_qf[3 * layer], got[i]).astype(BF).astype(F32)
         opened[layer, b] = jax.nn.sigmoid(query)
 
-    def f3(b, layer):
-        edge_finish(0, layer, b)
-
+    def tap_of(layer, rows, i):
+        return w_taps[layer, rows, i * LANES : (i + 1) * LANES]
+
+    lane_of = iota((ROWS, LANES), 1)
+
+    def f3_main(b, layer):
         def step(rows):
             signal = us[layer, b, rows, :].astype(F32)
-            extended = jnp.concatenate((edge_wide[0, rows, :], signal), axis=1)
+            extended = jnp.concatenate((jnp.zeros((ROWS, LANES), F32), signal), axis=1)
             total = jnp.zeros((ROWS, width), F32)
             for i in range(ntaps):
-                tap = w_taps[layer, rows, i * LANES : (i + 1) * LANES]
-                tap = jnp.concatenate([tap] * (width // LANES), axis=1)
+                tap = jnp.concatenate([tap_of(layer, rows, i)] * (width // LANES), axis=1)
                 moved = signal if i == 0 else pltpu.roll(extended, i, 1)[:, LANES:]
                 total = total + tap * moved
             convolved[layer, b, rows, :] = total
-            gs[layer, b, rows, :] = (opened[layer, b, rows, :] * total).astype(BF)
+            gated = opened[layer, b, rows, LANES:] * total[:, LANES:]
+            gs[layer, b, rows, LANES:] = gated.astype(BF)
+
+        in_rows(step)
+        if layer < last:
+            i = at(o_f, layer, b)
+            sent[i, :, LANES:] = nn(w_pt[3 * layer + 2], gs[layer, b, :, LANES:]).astype(BF)
+
+    def f3_edge(b, layer):
+        edge_finish(0, layer, b)
+
+        def step(rows):
+            before = edge_wide[0, rows, :]
+            more = jnp.zeros((ROWS, LANES), F32)
+            for i in range(1, ntaps):
+                more = more + tap_of(layer, rows, i) * pltpu.roll(before, i, 1)
+            total = convolved[layer, b, rows, :LANES] + jnp.where(lane_of < edge, more, 0.0)
+            convolved[layer, b, rows, :LANES] = total
+            gs[layer, b, rows, :LANES] = (opened[layer, b, rows, :LANES] * total).astype(BF)
 
         in_rows(step)
 
     def f3_send(b, layer):
         i = at(o_f, layer, b)
-        sent[i] = nn(w_pt[3 * layer + 2], gs[layer, b]).astype(BF)
+        if layer < last:
+            sent[i, :, :LANES] = nn(w_pt[3 * layer + 2], gs[layer, b, :, :LANES]).astype(BF)
+        else:
+            sent[i] = nn(w_pt[3 * layer + 2], gs[layer, b]).astype(BF)
         regroup_start(i)
 
     def f4(b, layer):
@@ -455,17 +491,14 @@
         sent[i] = nn(w_qb[3 * layer], ups[at(1, layer, b)]).astype(BF)
         regroup_start(i)
 
-    def b3(b, layer):
-        edge_finish(1, layer, b)
-
+    def b3_main(b, layer):
         def step(rows):
             conv_back = cb[b, rows, :]
-            extended = jnp.concatenate((conv_back, edge_wide[1, rows, :]), axis=1)
+            extended = jnp.concatenate((conv_back, jnp.zeros((ROWS, LANES), F32)), axis=1)
             signal = us[layer, b, rows, :].astype(F32)
             total = jnp.zeros((ROWS, width), F32)
             for i in range(ntaps):
-                tap = w_taps[layer, rows, i * LANES : (i + 1) * LANES]
-                tap = jnp.concatenate([tap] * (width // LANES), axis=1)
+                tap = jnp.concatenate([tap_of(layer, rows, i)] * (width // LANES), axis=1)
                 if i == 0:
                     moved = conv_back
                 else:
@@ -479,17 +512,37 @@
                 if b > 0:
                     narrow = narrow + tap_acc[rows, lanes]
                 tap_acc[rows, lanes] = narrow
-            ups[at(2, layer, b), rows, :] = total.astype(BF)
+            ups[at(2, layer, b), rows, :cut] = total[:, :cut].astype(BF)
+            back_tail[b, rows, :] = total[:, cut:]
 
         in_rows(step)
         i = at(u_b, layer, b)
-        sent[i] = nn(w_qb[3 * layer + 1], ups[at(2, layer, b)]).astype(BF)
+        upstream = ups[at(2, layer, b), :, :cut]
+        sent[i, :, :cut] = nn(w_qb[3 * layer + 1], upstream).astype(BF)
+
+    def b3_edge(b, layer):
+        edge_finish(1, layer, b)
+
+        def step(rows):
+            after = edge_wide[1, rows, :]
+            signal = us[layer, b, rows, cut:].astype(F32)
+            total = back_tail[b, rows, :]
+            for i in range(1, ntaps):
+                moved = jnp.where(lane_of >= LANES - edge, pltpu.roll(after, LANES - i, 1), 0.0)
+                total = total + tap_of(layer, rows, i) * moved
+                tap_acc[rows, i * LANES : (i + 1) * LANES] += moved * signal
+            ups[at(2, layer, b), rows, cut:] = total.astype(BF)
+
+        in_rows(step)
+        i = at(u_b, layer, b)
+        upstream = ups[at(2, layer, b), :, cut:]
+        sent[i, :, cut:] = nn(w_qb[3 * layer + 1], upstream).astype(BF)
         regroup_start(i)
 
     def b4(b, layer):
         regroup_copy(at(q_b, layer, b)).wait_recv()
+        back = nn(w_p[3 * layer], got[at(q_b, layer, b)])
         regroup_copy(at(u_b, layer, b)).wait_recv()
-        back = nn(w_p[3 * layer], got[at(q_b, layer, b)])
         back = back + nn(w_p[3 * layer + 1], got[at(u_b, layer, b)])
         before = cot[b].astype(F32) if layer == last else flow[b]
         if layer > 0:
@@ -553,8 +606,10 @@
         g_out[layer, :, 2 * pair :] = (first_q + first_u).astype(BF)
 
     constants_first()
+    loads[0].wait()
     make_pt(1)
     make_pt(0)
+    loads[1].wait()
     for b in both:
         f1_one(b, 0, 1, u_f)
         f1_one(b, 0, 0, q_f)
@@ -563,7 +618,9 @@
     for b in both:
         regroup_start(at(u_f, 0, b))
         regroup_start(at(q_f, 0, b))
+    loads[2].wait()
     make_q(3 * last + 2)
+    loads[3].wait()
     for b in both:
         b1(b, last)
     make_q(1)
@@ -577,21 +634,17 @@
                 make_p(3 * last + m)
         for b in both:
             f2_signal(b, layer)
-            if b == 0:
-                f2_query(b, layer)
-                if layer == last:
-                    b2_edge(b, layer)
-        for b in both:
-            if b > 0:
-                f2_query(b, layer)
-                if layer == last:
-                    b2_edge(b, layer)
-            f3(b, layer)
+            f2_query(b, layer)
+            if layer == last:
+                b2_edge(b, layer)
+                b3_main(b, layer)
+            f3_main(b, layer)
+            f3_edge(b, layer)
             if layer < last:
                 f3_send(b, layer)
             else:
                 b2_query(b, layer)
-                b3(b, layer)
+                b3_edge(b, layer)
         if layer < last:
             for m in range(3):
                 make_pt(3 * layer + 3 + m)
@@ -611,14 +664,11 @@
         f3_send(b, last)
     for layer in reversed(range(layers)):
         if layer < last:
-            b2_edge(0, layer)
-            b2_query(0, layer)
-            for b in range(1, batch):
+            for b in both:
                 b2_edge(b, layer)
-            for b in both:
-                if b > 0:
-                    b2_query(b, layer)
-                b3(b, layer)
+                b2_query(b, layer)
+                b3_main(b, layer)
+                b3_edge(b, layer)
         tap_rows(layer)
         if layer > 0:
             make_p(3 * layer - 1)
@@ -645,10 +695,18 @@
             pair_up(1)
             hand_back(2)
             pair_up(0)
+    term_q, term_u = None, None
     for b in both:
         regroup_copy(at(q_b, 0, b)).wait_recv()
+        more = nt(tok[b], got[at(q_b, 0, b)])
+        term_q = more if b == 0 else term_q + more
+        if b == batch - 1:
+            packed = nn(term_q.astype(BF) * c_mask1[...], c_pack1[0])
         regroup_copy(at(u_b, 0, b)).wait_recv()
-    grads_late(0)
+        more = nt(tok[b], got[at(u_b, 0, b)])
+        term_u = more if b == 0 else term_u + more
+    packed = packed + nn(term_u.astype(BF) * c_mask1[...], c_pack1[1])
+    g_out[0, :, 2 * pair :] = packed.astype(BF)
     late_scatter()
     for b in both:
         back = nn(w_p[0], got[at(q_b, 0, b)]) + nn(w_p[1], got[at(u_b, 0, b)])
@@ -740,6 +798,7 @@
         V((2 * layers * batch, 16, chan), BF),
         V((2 * layers * batch, 16, chan), BF),
         V((2, chan, LANES), F32),
+        V((batch, chan, LANES), F32),
         V((chan, ntaps * LANES), F32),
         V(grad, BF),
         V((layers, nz * share, projections * pair), BF),
@@ -754,6 +813,11 @@
         pltpu.SemaphoreType.DMA((2 * layers * batch,)),
         pltpu.SemaphoreType.DMA((4 * layers + 4,)),
         pltpu.SemaphoreType.DMA((4 * layers + 4,)),
+        V((batch, chan, width), BF),
+        V((batch, chan, width), BF),
+        V((many, chan, nb), BF),
+        V((many, chan, nb), BF),
+        pltpu.SemaphoreType.DMA((4,)),
     ]
     whole = pl.BlockSpec(memory_space=pltpu.VMEM)
     anywhere = pl.BlockSpec(memory_space=pl.ANY)
@@ -763,7 +827,7 @@
     moved = pl.pallas_call(
         functools.partial(kernel, dims),
         out_shape=(x_shape, jax.ShapeDtypeStruct(grad, BF), taps_shape),
-        in_specs=[whole] * 5,
+        in_specs=[anywhere] * 4 + [whole],
         out_specs=[whole] * 3,
         scratch_shapes=scratch,
         compiler_params=pltpu.CompilerParams(

time: 104 us -> 102 us (0.981)
  Pallas kernels: 103 us -> 101 us
    pallas_call x1, Pallas kernels: 99.6 us -> 97.9 us  [body(): pl.pallas_call(functools.partial(kernel, dims), out_shape=(x_shape, jax.S...]
where the time goes in v3:
time: 102 us
  Pallas kernels  101 us (99%)
    pallas_call x1, Pallas kernels, body(): pl.pallas_call(functools.partial(kernel, dims), out_shape=(x_shape, jax.S...  97.9 us
    pallas_call x1, Pallas kernels, body(): pl.pallas_call(functools.partial(unpack, nb, projections), out_shape=(x_s...  3.34 us

profile of v3, /device:TPU:1, one launch (start us, length us, event | category | flops | bytes accessed | tf_op | source)
XLA Modules:
  0.0 102.0 jit_solution(13258225735139747651)
XLA Ops:
  0.6 97.9 %shard_map.84 = (bf16[2,256,256]{2,1,0:T(8,128)(2,1)}, bf16[3,256,384]{2,1,0:T(8,128)(2,1)}, bf16[3,4,256]{2,1,0:T(4,128)(2,1)}) custom-call(bf16[2,256,256]{2,1,0:T(8,128)(2,1)} %tok_in.1, bf16[2,256,256]{2,1,0:T(8,128)(2,1)} %cot_in.1, bf16[9,256,64]{2,1,0:T(8,128)(2,1)} %bitcast.4, bf16[9,256,64]{2,1,0:T(8,128)(2,1)} %bitcast.5, bf16[3,4,256]{2,1,0:T(4,128)(2,1)} %taps.1), custom_call_target="tpu_custom_call" | custom-call | tf_op jit(solution)/shard_map/pallas_call | solution.py:827
  98.5 3.3 %shard_map.85 = (bf16[2,256,256]{2,1,0:T(8,128)(2,1)}, bf16[9,256,64]{2,1,0:T(8,128)(2,1)}, bf16[9,256,64]{2,1,0:T(8,128)(2,1)}, bf16[3,4,256]{2,1,0:T(4,128)(2,1)}) custom-call(bf16[2,256,256]{2,1,0:T(8,128)(2,1)} %get-tuple-element.11.x, bf16[3,256,384]{2,1,0:T(8,128)(2,1)} %get-tuple-element.12.sums, bf16[3,4,256]{2,1,0:T(4,128)(2,1)} %get-tuple-element.13.tap), custom_call_target="tpu_custom_call" | custom-call | tf_op jit(solution)/shard_map/pallas_call | solution.py:843

commit v4 on v3

--- a/solution.py
+++ b/solution.py
@@ -615,9 +615,9 @@
         f1_one(b, 0, 0, q_f)
     constants_second()
     pl.semaphore_wait(barrier, nh - 1 + parts - 1)
-    for b in both:
-        regroup_start(at(u_f, 0, b))
-        regroup_start(at(q_f, 0, b))
+    for kind in (u_f, q_f):
+        for b in both:
+            regroup_start(at(kind, 0, b))
     loads[2].wait()
     make_q(3 * last + 2)
     loads[3].wait()

time: 102 us -> 102 us (level)
  no operation moved by 1% of the time
where the time goes in v4:
time: 102 us
  Pallas kernels  101 us (99%)
    pallas_call x1, Pallas kernels, body(): pl.pallas_call(functools.partial(kernel, dims), out_shape=(x_shape, jax.S...  97.8 us
    pallas_call x1, Pallas kernels, body(): pl.pallas_call(functools.partial(unpack, nb, projections), out_shape=(x_s...  3.34 us

profile of v4, /device:TPU:1, one launch (start us, length us, event | category | flops | bytes accessed | tf_op | source)
XLA Modules:
  0.0 101.9 jit_solution(5789296865313425874)
XLA Ops:
  0.6 97.8 %shard_map.84 = (bf16[2,256,256]{2,1,0:T(8,128)(2,1)}, bf16[3,256,384]{2,1,0:T(8,128)(2,1)}, bf16[3,4,256]{2,1,0:T(4,128)(2,1)}) custom-call(bf16[2,256,256]{2,1,0:T(8,128)(2,1)} %tok_in.1, bf16[2,256,256]{2,1,0:T(8,128)(2,1)} %cot_in.1, bf16[9,256,64]{2,1,0:T(8,128)(2,1)} %bitcast.4, bf16[9,256,64]{2,1,0:T(8,128)(2,1)} %bitcast.5, bf16[3,4,256]{2,1,0:T(4,128)(2,1)} %taps.1), custom_call_target="tpu_custom_call" | custom-call | tf_op jit(solution)/shard_map/pallas_call | solution.py:827
  98.4 3.3 %shard_map.85 = (bf16[2,256,256]{2,1,0:T(8,128)(2,1)}, bf16[9,256,64]{2,1,0:T(8,128)(2,1)}, bf16[9,256,64]{2,1,0:T(8,128)(2,1)}, bf16[3,4,256]{2,1,0:T(4,128)(2,1)}) custom-call(bf16[2,256,256]{2,1,0:T(8,128)(2,1)} %get-tuple-element.11.x, bf16[3,256,384]{2,1,0:T(8,128)(2,1)} %get-tuple-element.12.sums, bf16[3,4,256]{2,1,0:T(4,128)(2,1)} %get-tuple-element.13.tap), custom_call_target="tpu_custom_call" | custom-call | tf_op jit(solution)/shard_map/pallas_call | solution.py:843
